TPU v7x, 32 devices: a whole 2x2x4 slice. The times are simulated.
32 devices in a mesh: grp: 2 (over y), gx: 4 (over z), gy: 4 (over x, core).
Axes of the slice: x: 2, y: 2, z: 4, core: 2. Of those that a mesh axis runs over, the one named last changes fastest.
Arguments:
- stream_in: bfloat16 [128, 8192], P(('grp', 'gy'), 'gx'), parts along dimension 0, may hold values from -0.59765625 to 0.59765625
- attention_gain: float32 [8192], P('gx'), may hold values from 0.1 to 1.9
- dense_gain: float32 [8192], P('gx'), may hold values from 0.1 to 1.9
- w_query: bfloat16 [8192, 8192], P('gx', 'gy'), may hold values from -0.0625 to 0.0625
- w_keyval: bfloat16 [8192, 1024], P('gx'), may hold values from -0.0625 to 0.0625
- w_out: bfloat16 [8192, 8192], P('gy', 'gx'), may hold values from -0.0625 to 0.0625
- gate_up: bfloat16 [8192, 2, 26624], P('gx', None, 'gy'), may hold values from -0.0625 to 0.0625
- cache_entries: bfloat16 [128, 2, 384, 512], P(('grp', 'gx', 'gy')), parts along dimension 0, as said below
- lengths: int32 [128], P(('grp', 'gx', 'gy')), parts along dimension 0, may hold values from 1 to 384, as said below
Outputs:
- stream: bfloat16 [128, 8192], P(('grp', 'gy'), 'gx'), parts along dimension 0
- mlp_hidden: bfloat16 [128, 26624], P(('grp', 'gx'), 'gy'), parts along dimension 0
- new_entries: bfloat16 [128, 1024], P(('grp', 'gx', 'gy')), parts along dimension 0
There are 2 independent parts, one for each index of `grp`. A program takes and returns all parts, laid end to end along the dimension named above; an argument that names none is the same for every part. Nothing has to cross between parts.
Inputs may be any that keep to these rules, and one draw needn't show every extreme that they name: `lengths`: cache slots at or past a row's length are never read; some row in every draw has exactly 384. `cache_entries`: keys are stored already rotated.
All inputs are finite; a program needn't handle non-finite values.
Results may differ from a plain program's by a relative error of at most 0.025.
The roundings to bfloat16 on the way count: a program that leaves them out, or rounds other values in their place, can miss the bound.
Values may be sent and summed in bfloat16 or wider, within the bound.
No kernel may reach another device: no remote copies, remote signals or barrier semaphores. Data moves between devices by JAX's collectives and lax.ppermute only.
A program may use at most 256 MiB of HBM per device.

v0:
```python
import math

import jax
import jax.numpy as jnp
from jax import lax
from jax.sharding import PartitionSpec as P

D = 8192
HD = 128
QH = 64
KVH = 4
CACHE = 384


rope_base = 500000.0
epsilon = 1e-05


def rotate(vectors, positions):
    half_dim = HD // 2
    frequency = jnp.exp(jnp.arange(half_dim, dtype=jnp.float32) * (-2.0 * math.log(rope_base) / HD))
    angles = positions.astype(jnp.float32)[:, None] * frequency[None, :]
    cosine = jnp.cos(angles)[:, None, :]
    sinus = jnp.sin(angles)[:, None, :]
    leading = vectors[..., :half_dim]
    trailing = vectors[..., half_dim:]
    return jnp.concatenate(
        [leading * cosine - trailing * sinus, trailing * cosine + leading * sinus], axis=-1
    )


def attend(query_rot, key_rot, value_new, cache_entries, lengths):
    row_total = query_rot.shape[0]
    group_size = QH // KVH
    grouped = query_rot.reshape(row_total, KVH, group_size, HD)
    score_scale = 1.0 / math.sqrt(HD)
    own_score = (
        jnp.einsum("rkgd,rkd->rkg", grouped, key_rot, preferred_element_type=jnp.float32)
        * score_scale
    )
    visible = (jnp.arange(CACHE, dtype=jnp.int32)[None, :] < lengths[:, None])[:, None, None, :]
    cached_keys = cache_entries[:, 0].reshape(row_total, CACHE, KVH, HD)
    scores = (
        jnp.einsum("rkgd,rtkd->rkgt", grouped, cached_keys, preferred_element_type=jnp.float32)
        * score_scale
    )
    highest = jnp.maximum(jnp.max(jnp.where(visible, scores, -jnp.inf), axis=3), own_score)
    expo_terms = jnp.where(visible, jnp.exp(scores - highest[..., None]), 0.0)
    own_weight = jnp.exp(own_score - highest)
    denominator = jnp.sum(expo_terms, axis=3) + own_weight
    rounded_w = expo_terms.astype(jnp.bfloat16)
    own_rounded = own_weight.astype(jnp.bfloat16).astype(jnp.float32)
    cached_values = cache_entries[:, 1].reshape(row_total, CACHE, KVH, HD)
    summed = jnp.einsum(
        "rkgt,rtkd->rkgd", rounded_w, cached_values, preferred_element_type=jnp.float32
    )
    summed = summed + own_rounded[..., None] * value_new.astype(jnp.float32)[:, :, None, :]
    return (summed / denominator[..., None]).astype(jnp.bfloat16).reshape(row_total, QH * HD)


def on_device(
    stream_in, attention_gain, dense_gain, w_query, w_keyval, w_out, gate_up, cache_entries, lengths
):
    gx_count = lax.axis_size("gx")
    gy_count = lax.axis_size("gy")
    width = stream_in.shape[1]
    device_rows = lengths.shape[0]
    keyval_width = w_keyval.shape[1] // 2
    stream_f = stream_in.astype(jnp.float32)
    square_one = lax.psum(jnp.sum(stream_f * stream_f, axis=1), "gx")
    scale_one = lax.rsqrt(square_one[:, None] / D + epsilon)
    normed = (stream_f * scale_one * attention_gain[None, :]).astype(jnp.bfloat16)
    gathered = lax.all_gather(normed, "gy", axis=0, tiled=True)
    piece_rows = gathered
    queries = lax.psum_scatter(
        jnp.dot(piece_rows, w_query, preferred_element_type=jnp.float32),
        "gx",
        scatter_dimension=0,
        tiled=True,
    ).astype(jnp.bfloat16)
    picked = gathered.reshape(gx_count, gy_count, device_rows, width)
    picked = lax.dynamic_index_in_dim(picked, lax.axis_index("gy"), 1, keepdims=False).reshape(
        gx_count * device_rows, width
    )
    piece_rows = picked
    keyval = lax.psum_scatter(
        jnp.dot(piece_rows, w_keyval, preferred_element_type=jnp.float32).astype(jnp.bfloat16),
        "gx",
        scatter_dimension=0,
        tiled=True,
    )
    query_rows = lax.all_to_all(queries, "gy", split_axis=0, concat_axis=1, tiled=True)
    query_rot = rotate(query_rows.astype(jnp.float32).reshape(device_rows, -1, HD), lengths).astype(
        jnp.bfloat16
    )
    key_rot = rotate(
        keyval[:, :keyval_width].astype(jnp.float32).reshape(device_rows, -1, HD), lengths
    ).astype(jnp.bfloat16)
    value_new = keyval[:, keyval_width:]
    new_entries = jnp.concatenate([key_rot.reshape(device_rows, keyval_width), value_new], axis=1)
    context = attend(
        query_rot, key_rot, value_new.reshape(device_rows, -1, HD), cache_entries, lengths
    )
    head_rows = lax.all_to_all(context, "gy", split_axis=1, concat_axis=0, tiled=True)
    partial_out = jnp.dot(
        lax.all_gather(head_rows, "gx", axis=0, tiled=True),
        w_out,
        preferred_element_type=jnp.float32,
    )
    attended = lax.psum_scatter(
        partial_out.astype(jnp.bfloat16), "gy", scatter_dimension=0, tiled=True
    ).astype(jnp.float32)
    residual = stream_f + attended
    stream = residual.astype(jnp.bfloat16)
    square_two = lax.psum(jnp.sum(residual * residual, axis=1), "gx")
    normed_two = (
        residual * lax.rsqrt(square_two[:, None] / D + epsilon) * dense_gain[None, :]
    ).astype(jnp.bfloat16)
    mlp_in = lax.all_gather(normed_two, "gy", axis=0, tiled=True)
    hidden_cols = gate_up.shape[2]
    weights = gate_up.reshape(width, 2 * hidden_cols)
    projected = lax.psum_scatter(
        jnp.dot(mlp_in, weights, preferred_element_type=jnp.float32).astype(jnp.bfloat16),
        "gx",
        scatter_dimension=0,
        tiled=True,
    ).astype(jnp.float32)
    mlp_hidden = (jax.nn.silu(projected[:, :hidden_cols]) * projected[:, hidden_cols:]).astype(
        jnp.bfloat16
    )
    return (stream, mlp_hidden, new_entries)


def solution(mesh):
    placed = (
        P(("grp", "gy"), "gx"),
        P("gx"),
        P("gx"),
        P("gx", "gy"),
        P("gx", None),
        P("gy", "gx"),
        P("gx", None, "gy"),
        P(("grp", "gx", "gy"), None, None, None),
        P(("grp", "gx", "gy")),
    )
    return jax.shard_map(
        on_device,
        mesh=mesh,
        in_specs=placed,
        out_specs=(P(("grp", "gy"), "gx"), P(("grp", "gx"), "gy"), P(("grp", "gx", "gy"), None)),
        check_vma=False,
    )
```

profile of v0, /device:TPU:0, one launch (start us, length us, event | category | flops | bytes accessed | tf_op | source)
XLA Modules:
  0.0 215.1 jit_solution(10101012307544464383)
XLA Ops:
  7.2 1.0 fusion.9
  8.2 13.5 %psum.14 = f32[16]{0:T(128)S(1)} all-reduce(f32[16]{0:T(128)S(1)} %fusion.9), channel_id=1, replica_groups=mesh['grp'=2,'gx'=4,'gy'=4] {'gx'}, use_global_device_ids=true, to_apply=%region_1.0 | all-reduce | flops 16 | bytes 128 | tf_op jit(solution)/shard_map/psum | solution.py:70
  21.6 0.9 fusion.11
  22.6 5.8 %all_gather.9 = bf16[64,2048]{1,0:T(8,128)(2,1)S(1)} all-gather(bf16[16,2048]{1,0:T(8,128)(2,1)S(1)} %fusion.11), channel_id=1, replica_groups=mesh['grp'=2,'gx'=4,'gy'=4] {'gy'}, dimensions={0}, use_global_device_ids=true | all-gather | bytes 327680 | tf_op jit(solution)/shard_map/all_gather | solution.py:73
  28.4 5.8 %fusion.21 = f32[64,2048]{1,0:T(8,128)} fusion(bf16[64,2048]{1,0:T(8,128)(2,1)S(1)} %all_gather.9, bf16[2048,2048]{1,0:T(8,128)(2,1)} %param.12), kind=kOutput, calls=%fused_computation.53 | convolution fusion | flops 536870912 | bytes 9175040 | tf_op jit(solution)/shard_map/dot_general | solution.py:76
  34.3 2.8 %convolution_convert_fusion.2 = bf16[16,1024]{1,0:T(8,128)(2,1)S(1)} fusion(bf16[16,2048]{1,0:T(8,128)(2,1)S(1)} %reshape.131, bf16[2048,1024]{1,0:T(8,128)(2,1)} %param.13), kind=kOutput, calls=%fused_computation.6 | convolution fusion | flops 67125248 | bytes 4292608 | tf_op jit(solution)/shard_map/dot_general | solution.py:87
  37.2 16.5 %all-reduce = bf16[16,1024]{1,0:T(8,128)(2,1)S(1)} all-reduce(bf16[16,1024]{1,0:T(8,128)(2,1)S(1)} %convolution_convert_fusion.2), channel_id=3, replica_groups=mesh['grp'=2,'gx'=4,'gy'=4] {'gx'}, use_global_device_ids=true, to_apply=%region_4.5.clone | all-reduce | flops 16384 | bytes 65536
  55.4 3.3 %fusion.19 = (bf16[4,1,384,512]{3,2,1,0:T(8,128)(2,1)S(1)}, bf16[4,1,384,512]{3,2,1,0:T(8,128)(2,1)}) fusion(bf16[4,2,384,512]{3,2,1,0:T(8,128)(2,1)} %param.16), kind=kLoop, calls=%fused_computation.51 | loop fusion | bytes 6291456 | tf_op jit(solution)/shard_map/slice | solution.py:42
  58.7 0.9 convert_element_type.81
  60.3 3.3 %all-to-all-start = ((bf16[4,4,2048]{2,1,0:T(4,128)(2,1)}), bf16[4,4,2048]{2,1,0:T(4,128)(2,1)S(1)}, u32[]{:S(2)}, u32[]{:S(2)}) async-start(bf16[4,4,2048]{2,1,0:T(4,128)(2,1)} %all_to_all.24), calls=%async_computation.1 | async-start | bytes 131072 | tf_op jit(solution)/shard_map/all_to_all | solution.py:92
  63.7 0.9 copy.28
  64.6 1.9 copy.29
  66.5 1.2 all-to-all-done
  69.8 6.5 %all_to_all.32 = bf16[4,4,2048]{2,0,1:T(4,128)(2,1)S(1)} all-to-all(bf16[4,4,2048]{2,0,1:T(4,128)(2,1)S(1)} %copy.23), channel_id=1, replica_groups=mesh['grp'=2,'gx'=4,'gy'=4] {'gy'}, dimensions={1} | all-to-all | bytes 131072 | tf_op jit(solution)/shard_map/all_to_all | solution.py:104
  76.3 14.5 %all_gather.10 = bf16[64,2048]{1,0:T(8,128)(2,1)S(1)} all-gather(bf16[16,2048]{1,0:T(8,128)(2,1)S(1)} %all_to_all.29), channel_id=1, replica_groups=mesh['grp'=2,'gx'=4,'gy'=4] {'gx'}, dimensions={0}, use_global_device_ids=true | all-gather | bytes 327680 | tf_op jit(solution)/shard_map/all_gather | solution.py:106
  90.8 5.7 %convolution_convert_fusion.1 = bf16[64,2048]{1,0:T(8,128)(2,1)} fusion(bf16[64,2048]{1,0:T(8,128)(2,1)S(1)} %all_gather.10, bf16[2048,2048]{1,0:T(8,128)(2,1)} %param.14), kind=kOutput, calls=%fused_computation.1 | convolution fusion | flops 537001984 | bytes 8912896 | tf_op jit(solution)/shard_map/dot_general | solution.py:105
  96.5 36.9 %copy.30 = bf16[256,8,2,6656]{3,1,2,0:T(8,128)(2,1)} copy(bf16[256,8,2,6656]{3,2,1,0:T(2,128)(2,1)} %bitcast.32) | data formatting | bytes 109051904
  133.5 1.0 multiply_reduce_fusion
  134.4 9.2 %psum.15 = f32[16]{0:T(128)S(1)} all-reduce(f32[16]{0:T(128)S(1)} %multiply_reduce_fusion), channel_id=1, replica_groups=mesh['grp'=2,'gx'=4,'gy'=4] {'gx'}, use_global_device_ids=true, to_apply=%region_8.9 | all-reduce | flops 16 | bytes 128 | tf_op jit(solution)/shard_map/psum | solution.py:115
  143.7 1.5 multiply_convert_fusion
  145.2 5.8 %all_gather.11 = bf16[64,2048]{1,0:T(8,128)(2,1)S(1)} all-gather(bf16[16,2048]{1,0:T(8,128)(2,1)S(1)} %get-tuple-element.7), channel_id=1, replica_groups=mesh['grp'=2,'gx'=4,'gy'=4] {'gy'}, dimensions={0}, use_global_device_ids=true | all-gather | bytes 327680 | tf_op jit(solution)/shard_map/all_gather | solution.py:119
  151.0 20.6 %convolution_convert_fusion = bf16[64,13312]{1,0:T(8,128)(2,1)} fusion(bf16[64,2048]{1,0:T(8,128)(2,1)S(1)} %all_gather.11, bf16[2048,13312]{1,0:T(8,128)(2,1)} %bitcast.31), kind=kOutput, calls=%fused_computation | convolution fusion | flops 3490512896 | bytes 56492032 | tf_op jit(solution)/shard_map/dot_general | solution.py:123
  172.3 34.5 %reduce-scatter.8.cloned.1.call-done = bf16[16,13312]{1,0:T(8,128)(2,1)} async-done(((bf16[64,13312]{1,0:T(8,128)(2,1)}), bf16[16,13312]{1,0:T(8,128)(2,1)}) %reduce-scatter.8.cloned.1.call-update) | async-done | bytes 426000 | tf_op jit(solution)/shard_map/reduce_scatter | solution.py:122
  206.7 1.1 convert_element_type.99
  (49 shorter events, 5.7 us)
Async XLA Ops:
  7.2 51.5 %reduce-scatter.4.cloned.1.call-start = ((), (), s32[]{:S(2)}) async-start(), calls=%async_computation.5 | async-start | bytes 655360 | tf_op jit(solution)/shard_map/reduce_scatter | solution.py:75
  34.1 19.6 %copy-start.3 = (u32[32]{0:T(128)S(1)}, u32[32]{0:T(128)}, u32[]{:S(2)}) copy-start(u32[32]{0:T(128)} %constant.32) | copy-start | bytes 388
  34.1 20.9 %copy-start.2 = (s32[4]{0:T(128)S(1)}, s32[4]{0:T(128)}, u32[]{:S(2)}) copy-start(s32[4]{0:T(128)} %param.17) | copy-start | bytes 52
  60.3 7.4 %all-to-all-start = ((bf16[4,4,2048]{2,1,0:T(4,128)(2,1)}), bf16[4,4,2048]{2,1,0:T(4,128)(2,1)S(1)}, u32[]{:S(2)}, u32[]{:S(2)}) async-start(bf16[4,4,2048]{2,1,0:T(4,128)(2,1)} %all_to_all.24), calls=%async_computation.1 | async-start | bytes 131072 | tf_op jit(solution)/shard_map/all_to_all | solution.py:92
  63.6 69.9 %reduce-scatter.6.cloned.1.call-start = ((), (), s32[]{:S(2)}) async-start(), calls=%async_computation.6 | async-start | bytes 327680 | tf_op jit(solution)/shard_map/reduce_scatter | solution.py:110
  96.5 110.3 %reduce-scatter.8.cloned.1.call-start = ((), (), s32[]{:S(2)}) async-start(), calls=%async_computation.7 | async-start | bytes 2129920 | tf_op jit(solution)/shard_map/reduce_scatter | solution.py:122
  96.5 37.0 %copy-start = (bf16[16,2048]{1,0:T(8,128)(2,1)S(1)}, bf16[16,2048]{1,0:T(8,128)(2,1)}, u32[]{:S(2)}) copy-start(bf16[16,2048]{1,0:T(8,128)(2,1)} %param.9) | copy-start | bytes 196612
  96.5 47.2 %copy-start.1 = (f32[2048]{0:T(1024)S(1)}, f32[2048]{0:T(1024)}, u32[]{:S(2)}) copy-start(f32[2048]{0:T(1024)} %param.11) | copy-start | bytes 24580
Sparse Core Ops, SparseCore 0:
  34.3 20.4 reduce-scatter.3
  96.6 17.4 reduce-scatter.5
  171.7 34.9 reduce-scatter.7
where the time goes:
time: 216 us; the launch traced here: 215 us
  blocking collectives  71.7 us (33%)
  local copies, waits for them, and re-layouts  44.8 us (21%)
  matrix products  36.3 us (17%)
  waiting for transfers between devices  35.7 us (17%)
  between operations  14.6 us (7%)
  other arithmetic  8.67 us (4%)
  starting transfers between devices  3.41 us (2%)
    unnamed x13, local copies, waits for them, and re-layouts  40.3 us
    reduce_scatter x1, waiting for transfers between devices, on_device(): lax.psum_scatter(jnp.dot(mlp_in, weights, preferred_element_type=jnp.floa...  34.5 us
    dot_general x1, matrix products, on_device(): jnp.dot(mlp_in, weights, preferred_element_type=jnp.float32)  20.6 us
    unnamed x1, blocking collectives  16.5 us
    all_gather x1, blocking collectives, on_device(): lax.all_gather(head_rows, 'gx', axis=0, tiled=True)  14.5 us
    psum x1, blocking collectives, on_device(): square_one = lax.psum(jnp.sum(stream_f * stream_f, axis=1), 'gx')  13.5 us
    psum x1, blocking collectives, on_device(): square_two = lax.psum(jnp.sum(residual * residual, axis=1), 'gx')  9.25 us
    all_to_all x1, blocking collectives, on_device(): lax.all_to_all(context, 'gy', split_axis=1, concat_axis=0, tiled=True)  6.49 us
  transfers between devices with their start and end apart: 4, of which 2 were waited for; matrix products, arithmetic and copies ran while one was open for 22% of the time, Pallas kernels for 0%

commit v1 on v0

v1 whole, which is shorter than its diff:
```python
import functools
import math

import jax
import jax.numpy as jnp
from jax import lax
from jax.experimental import pallas as pl
from jax.experimental.pallas import tpu as pltpu
from jax.sharding import PartitionSpec as P

D = 8192
HD = 128
QH = 64
KVH = 4
CACHE = 384


rope_base = 500000.0
epsilon = 1e-05

VMEM_BYTES = 58 * 1024 * 1024
LANES = 128
f32 = jnp.float32
bf16 = jnp.bfloat16


def call(kernel, name, flops, moved, **kwargs):
    return pl.pallas_call(
        kernel,
        name=name,
        compiler_params=pltpu.CompilerParams(vmem_limit_bytes=VMEM_BYTES),
        cost_estimate=pl.CostEstimate(flops=flops, bytes_accessed=moved, transcendentals=0),
        **kwargs,
    )


def side_tile(sums):
    lane = lax.broadcasted_iota(jnp.int32, (sums.shape[0], LANES), 1)
    first = sums.astype(bf16).astype(f32)
    second = (sums - first).astype(bf16).astype(f32)
    third = sums - first - second
    tile = jnp.where(lane == 0, first, jnp.where(lane == 1, second, third))
    return jnp.where(lane < 3, tile, 0.0).astype(bf16)


def qkv_kernel(which, rows, gain, w_query, w_keyval, parcel, left, *, steps, cut):
    step = pl.program_id(0)
    count = rows.shape[0]
    device_rows = parcel.shape[1]
    query_cols = steps * cut
    keyval_cols = w_keyval.shape[1]

    def put(values, start, size):
        for place in range(parcel.shape[0]):
            parcel[place, :, pl.ds(start, size)] = values[
                place * device_rows : (place + 1) * device_rows
            ].astype(bf16)

    def product(weights):
        both = jnp.dot(left[...], weights, preferred_element_type=f32)
        return both[:count] + both[count:]

    @pl.when(step == 0)
    def _():
        wide = rows[...].astype(f32)
        gained = wide * gain[...]
        coarse = gained.astype(bf16)
        left[:count] = coarse
        left[count:] = (gained - coarse.astype(f32)).astype(bf16)
        squares = jnp.sum(wide * wide, axis=1, keepdims=True)
        put(side_tile(squares).astype(f32), query_cols + keyval_cols, LANES)
        put(product(w_keyval[...]), query_cols, keyval_cols)

    put(product(w_query[...]), pl.multiple_of(step * cut, LANES), cut)


def project_qkv(rows, gain, w_query, w_keyval, gy_count, places, device_rows):
    count, width = rows.shape
    query_cols = w_query.shape[1]
    keyval_cols = w_keyval.shape[1] // gy_count
    cut = min(512, query_cols)
    steps = query_cols // cut
    parcel_cols = query_cols + keyval_cols + LANES
    index = lax.axis_index("gy").astype(jnp.int32).reshape(1)
    return call(
        functools.partial(qkv_kernel, steps=steps, cut=cut),
        "qkv",
        4 * count * width * (query_cols + keyval_cols),
        2 * width * (query_cols + keyval_cols),
        grid_spec=pltpu.PrefetchScalarGridSpec(
            num_scalar_prefetch=1,
            grid=(steps,),
            in_specs=[
                pl.BlockSpec((count, width), lambda n, s: (0, 0)),
                pl.BlockSpec((1, width), lambda n, s: (0, 0)),
                pl.BlockSpec((width, cut), lambda n, s: (0, n)),
                pl.BlockSpec((width, keyval_cols), lambda n, s: (0, s[0])),
            ],
            out_specs=pl.BlockSpec((places, device_rows, parcel_cols), lambda n, s: (0, 0, 0)),
            scratch_shapes=[pltpu.VMEM((2 * count, width), bf16)],
        ),
        out_shape=jax.ShapeDtypeStruct((places, device_rows, parcel_cols), bf16),
    )(index, rows, gain.reshape(1, width), w_query, w_keyval)


def attend_kernel(
    arrived, cosine, sinus, lengths, cache, context, entries, *, gx_count, gy_count, query_cols
):
    head = pl.program_id(0)
    device_rows = arrived.shape[1]
    keyval_cols = 2 * KVH * HD // gy_count
    heads_in = query_cols // HD
    parcels = gy_count // KVH
    blocks_in = keyval_cols // HD
    group = parcels * heads_in
    total = group * device_rows

    def summed(parcel, start, size):
        values = arrived[parcel, :, pl.ds(start, size)].astype(f32)
        for block in range(1, gx_count):
            values = values + arrived[block * gy_count + parcel, :, pl.ds(start, size)].astype(f32)
        return values

    squares = jnp.sum(summed(0, query_cols + keyval_cols, LANES), axis=1, keepdims=True)
    scale = lax.rsqrt(squares / D + epsilon)

    def taken(parcel, start, size):
        return (summed(parcel, start, size) * scale).astype(bf16).astype(f32)

    def turned(values, cosines, sines):
        return values * cosines + pltpu.roll(values, HD // 2, 1) * sines

    def keyval_block(number):
        start = query_cols + (number % blocks_in) * HD
        return taken(number // blocks_in, pl.multiple_of(start, LANES), HD)

    def spread(values):
        return jnp.concatenate([values] * group, axis=0)

    pieces = []
    for parcel in range(parcels):
        values = taken(head * parcels + parcel, 0, query_cols)
        pieces += [values[:, n * HD : (n + 1) * HD] for n in range(heads_in)]
    query_rot = turned(jnp.concatenate(pieces, axis=0), cosine[...], sinus[...]).astype(bf16)
    key_rot = turned(keyval_block(head), cosine[:device_rows], sinus[:device_rows]).astype(bf16)
    value_new = keyval_block(KVH + head)
    entries[:, pl.ds(pl.multiple_of(head * HD, LANES), HD)] = key_rot
    entries[:, pl.ds(pl.multiple_of((KVH + head) * HD, LANES), HD)] = value_new.astype(bf16)

    score_scale = 1.0 / math.sqrt(HD)
    own = jnp.sum(query_rot.astype(f32) * spread(key_rot.astype(f32)), axis=1, keepdims=True)
    own = own * score_scale
    row_of = lax.broadcasted_iota(jnp.int32, (total, CACHE), 0) % device_rows
    slot = lax.broadcasted_iota(jnp.int32, (total, CACHE), 1)
    scores = jnp.zeros((total, CACHE), f32)
    for row in range(device_rows):
        found = lax.dot_general(
            query_rot, cache[row, 0], (((1,), (1,)), ((), ())), preferred_element_type=f32
        )
        scores = jnp.where(row_of == row, found, scores)
    scores = jnp.where(slot < lengths[...], scores * score_scale, -jnp.inf)
    top = jnp.maximum(jnp.max(scores, axis=1, keepdims=True), own)
    terms = jnp.exp(scores - top)
    own_weight = jnp.exp(own - top)
    denominator = jnp.sum(terms, axis=1, keepdims=True) + own_weight
    gathered = own_weight.astype(bf16).astype(f32) * spread(value_new)
    for row in range(device_rows):
        weights = jnp.where(row_of == row, terms, 0.0).astype(bf16)
        gathered = gathered + jnp.dot(weights, cache[row, 1], preferred_element_type=f32)
    result = gathered / denominator
    for parcel in range(parcels):
        for n in range(heads_in):
            first = (parcel * heads_in + n) * device_rows
            context[parcel, :, n * HD : (n + 1) * HD] = result[first : first + device_rows].astype(
                bf16
            )


def attend(arrived, cache_entries, lengths, gx_count, gy_count, query_cols):
    device_rows = lengths.shape[0]
    group = QH // KVH
    half_dim = HD // 2
    frequency = jnp.exp(jnp.arange(half_dim, dtype=f32) * (-2.0 * math.log(rope_base) / HD))
    angles = lengths.astype(f32)[:, None] * frequency[None, :]
    cosine = jnp.cos(angles)
    sinus = jnp.sin(angles)
    cosine = jnp.tile(jnp.concatenate([cosine, cosine], axis=1), (group, 1))
    sinus = jnp.tile(jnp.concatenate([-sinus, sinus], axis=1), (group, 1))
    limits = jnp.tile(lengths.reshape(device_rows, 1), (group, 1))
    total = group * device_rows
    parcels = gy_count // KVH
    return call(
        functools.partial(
            attend_kernel, gx_count=gx_count, gy_count=gy_count, query_cols=query_cols
        ),
        "attend",
        4 * total * HD * CACHE * KVH * device_rows,
        2 * cache_entries.size,
        grid=(KVH,),
        in_specs=[
            pl.BlockSpec(arrived.shape, lambda k: (0, 0, 0)),
            pl.BlockSpec((total, HD), lambda k: (0, 0)),
            pl.BlockSpec((total, HD), lambda k: (0, 0)),
            pl.BlockSpec((total, 1), lambda k: (0, 0)),
            pl.BlockSpec((device_rows, 2, CACHE, HD), lambda k: (0, 0, 0, k)),
        ],
        out_specs=[
            pl.BlockSpec((parcels, device_rows, query_cols), lambda k: (k, 0, 0)),
            pl.BlockSpec((device_rows, 2 * KVH * HD), lambda k: (0, 0)),
        ],
        out_shape=[
            jax.ShapeDtypeStruct((gy_count, device_rows, query_cols), bf16),
            jax.ShapeDtypeStruct((device_rows, 2 * KVH * HD), bf16),
        ],
    )(arrived, cosine, sinus, limits, cache_entries)


def out_kernel(rows, weights, result):
    result[...] = jnp.dot(rows[...], weights[...], preferred_element_type=f32)


def project_out(rows, weights):
    count, width = rows.shape
    cols = weights.shape[1]
    cut = min(512, cols)
    return call(
        out_kernel,
        "out",
        2 * count * width * cols,
        2 * width * cols,
        grid=(cols // cut,),
        in_specs=[
            pl.BlockSpec((count, width), lambda n: (0, 0)),
            pl.BlockSpec((width, cut), lambda n: (0, n)),
        ],
        out_specs=pl.BlockSpec((count, cut), lambda n: (0, n)),
        out_shape=jax.ShapeDtypeStruct((count, cols), f32),
    )(rows, weights)


def sum_and_spread(partial_out, stream_in, rows_in, dense_gain):
    gy_count = lax.axis_size("gy")
    gy_index = lax.axis_index("gy")
    width = partial_out.shape[1]

    def gained_rows(residual):
        squares = jnp.sum(residual * residual, axis=1, keepdims=True)
        gained = (residual * dense_gain[None, :]).astype(bf16)
        return jnp.concatenate([gained, side_tile(squares)], axis=1)

    if gy_count != 4:
        blocks = partial_out.astype(bf16).reshape(gy_count, -1, width)
        blocks = lax.all_to_all(blocks, "gy", split_axis=0, concat_axis=0, tiled=True)
        residual = stream_in.astype(f32) + jnp.sum(blocks.astype(f32), axis=0)
        gathered = lax.all_gather(gained_rows(residual), "gy", axis=0, tiled=True)
        return residual.astype(bf16), gathered

    core = gy_index % 2
    chip = gy_index // 2
    core_pairs = [(0, 1), (1, 0), (2, 3), (3, 2)]
    chip_pairs = [(0, 2), (2, 0), (1, 3), (3, 1)]

    def halves(values):
        blocks = values.reshape(2, 2, -1, width)
        first = blocks[:, 0].reshape(-1, width)
        second = blocks[:, 1].reshape(-1, width)
        return first, second

    first, second = halves(partial_out)
    sent = jnp.where(core == 0, second, first).astype(bf16)
    pair_sum = jnp.where(core == 0, first, second) + lax.ppermute(sent, "gy", core_pairs).astype(f32)
    other = lax.ppermute(pair_sum.astype(bf16), "gy", chip_pairs).astype(f32)
    first, second = halves(rows_in)
    residual = jnp.where(core == 0, first, second).astype(f32) + (pair_sum + other)
    count = stream_in.shape[0]
    stream = jnp.where(chip == 0, residual[:count], residual[count:]).astype(bf16)
    mine = gained_rows(residual)
    theirs = lax.ppermute(mine, "gy", core_pairs)
    even = jnp.where(core == 0, mine, theirs)
    odd = jnp.where(core == 0, theirs, mine)
    gathered = jnp.concatenate([even[:count], odd[:count], even[count:], odd[count:]], axis=0)
    return stream, gathered


def mlp_kernel(rows, weights, *rest, steps, side):
    results, total = rest[:-1], rest[-1]
    step = pl.program_id(0)
    depth, tiles = weights.shape[0], weights.shape[1]
    block = weights[...].reshape(depth, tiles * 2 * LANES)
    product = jnp.dot(rows[:, :depth], block, preferred_element_type=f32)

    @pl.when(step == 0)
    def _():
        total[...] = product

    @pl.when(step > 0)
    def _():
        total[...] += product

    @pl.when(step == steps - 1)
    def _():
        size = results[0].shape[0]
        for place, result in enumerate(results):
            result[:, : tiles * 2 * LANES] = total[place * size : (place + 1) * size].astype(bf16)


def gate_up_part(rows, view, part, tiles, places):
    count = rows.shape[0]
    width = view.shape[0]
    cols = tiles * 2 * LANES
    depth = min(512, width)
    steps = width // depth
    return call(
        functools.partial(mlp_kernel, steps=steps, side=0),
        "gate_up_%d" % part,
        2 * count * width * cols,
        2 * width * cols,
        grid=(steps,),
        in_specs=[
            pl.BlockSpec((count, depth), lambda k: (0, k)),
            pl.BlockSpec((depth, tiles, 2, LANES), lambda k: (k, part, 0, 0)),
        ],
        out_specs=[pl.BlockSpec((count // places, cols), lambda k: (0, 0))] * places,
        out_shape=[jax.ShapeDtypeStruct((count // places, cols), bf16)] * places,
        scratch_shapes=[pltpu.VMEM((count, cols), f32)],
    )(rows, view)


def hidden_kernel(sides, *refs, parts, places):
    result = refs[-1]
    squares = jnp.zeros((sides.shape[1], 1), f32)
    for place in range(places):
        squares = squares + jnp.sum(sides[place].astype(f32), axis=1, keepdims=True)
    scale = lax.rsqrt(squares / D + epsilon)
    start = 0
    for part in range(parts):
        blocks = refs[part * places : (part + 1) * places]
        tiles = blocks[0].shape[1] // (2 * LANES)
        for tile in range(tiles):
            def added(first):
                values = blocks[0][:, first : first + LANES].astype(f32)
                for block in blocks[1:]:
                    values = values + block[:, first : first + LANES].astype(f32)
                return values * scale

            gate = added(tile * 2 * LANES)
            up = added(tile * 2 * LANES + LANES)
            hidden = gate / (1.0 + jnp.exp(-gate)) * up
            result[:, start : start + LANES] = hidden.astype(bf16)
            start += LANES


def exchange(blocks):
    count = len(blocks)
    arrived = [blocks[0]]
    for shift in range(1, count):
        pairs = [(n, (n + shift) % count) for n in range(count)]
        arrived.append(lax.ppermute(blocks[shift], "gx", pairs))
    return arrived


def on_device(
    stream_in, attention_gain, dense_gain, w_query, w_keyval, w_out, gate_up, cache_entries, lengths
):
    gx_count = lax.axis_size("gx")
    gy_count = lax.axis_size("gy")
    gx_index = lax.axis_index("gx")
    width = stream_in.shape[1]
    device_rows = lengths.shape[0]
    query_cols = w_query.shape[1]
    hidden_cols = gate_up.shape[2]
    places = gx_count * gy_count

    rows_in = lax.all_gather(stream_in, "gy", axis=0, tiled=True)
    parcel = project_qkv(
        rows_in, attention_gain, w_query, w_keyval, gy_count, places, device_rows
    )
    arrived = lax.all_to_all(parcel, ("gx", "gy"), split_axis=0, concat_axis=0, tiled=True)
    context, new_entries = attend(
        arrived, cache_entries, lengths, gx_count, gy_count, query_cols
    )
    blocks = jnp.broadcast_to(context[None], (gx_count,) + context.shape)
    blocks = blocks.reshape((places,) + context.shape[1:])
    head_rows = lax.all_to_all(blocks, ("gx", "gy"), split_axis=0, concat_axis=0, tiled=True)
    partial_out = project_out(head_rows.reshape(places * device_rows, query_cols), w_out)
    stream, gathered = sum_and_spread(partial_out, stream_in, rows_in, dense_gain)

    count = gathered.shape[0]
    size = count // gx_count
    turned = lax.dynamic_slice_in_dim(
        jnp.concatenate([gathered, gathered], axis=0), gx_index * size, count, 0
    )
    tiles = hidden_cols // LANES
    view = jnp.swapaxes(gate_up.reshape(width, 2, tiles, LANES), 1, 2)
    cut = 13 if tiles % 13 == 0 else 1
    parts = tiles // cut
    sides = exchange([turned[n * size : (n + 1) * size, width:] for n in range(gx_count)])
    received = []
    for part in range(parts):
        made = gate_up_part(turned, view, part, cut, gx_count)
        received += exchange(made)
    mlp_hidden = call(
        functools.partial(hidden_kernel, parts=parts, places=gx_count),
        "hidden",
        8 * size * hidden_cols * gx_count,
        4 * size * hidden_cols * gx_count,
        out_shape=jax.ShapeDtypeStruct((size, hidden_cols), bf16),
    )(jnp.stack(sides, axis=0), *received)
    return (stream, mlp_hidden, new_entries)


def solution(mesh):
    placed = (
        P(("grp", "gy"), "gx"),
        P("gx"),
        P("gx"),
        P("gx", "gy"),
        P("gx", None),
        P("gy", "gx"),
        P("gx", None, "gy"),
        P(("grp", "gx", "gy"), None, None, None),
        P(("grp", "gx", "gy")),
    )
    return jax.shard_map(
        on_device,
        mesh=mesh,
        in_specs=placed,
        out_specs=(P(("grp", "gy"), "gx"), P(("grp", "gx"), "gy"), P(("grp", "gx", "gy"), None)),
        check_vma=False,
    )
```

time: 216 us -> 137 us (0.63)
  blocking collectives: 71.7 us -> 8.81 us
  Pallas kernels: 0 us -> 51.4 us
  local copies, waits for them, and re-layouts: 44.8 us -> 5.92 us
  matrix products: 36.3 us -> 0 us
  starting transfers between devices: 3.41 us -> 31.6 us
  between operations: 14.6 us -> 0.99 us
  other arithmetic: 8.67 us -> 4 us
    pallas_call x0 -> x8, Pallas kernels: none -> 51.4 us  [the longest x4 31.3 us: gate_up_part(): call(functools.partial(mlp_kernel, steps=steps, side=0), 'gate_up_%d' % p...]
    unnamed x13 -> x51, local copies, waits for them, and re-layouts: 40.3 us -> 0.78 us
    dot_general x7 -> x0, matrix products: 36.3 us -> none  [the longest x1 20.6 us: on_device(): jnp.dot(mlp_in, weights, preferred_element_type=jnp.float32)]
    reduce_scatter x3 -> x0, waiting for transfers between devices: 34.5 us -> none  [the longest x1 34.5 us: on_device(): lax.psum_scatter(jnp.dot(mlp_in, weights, preferred_element_type=jnp.floa...]
    ppermute x0 -> x18, starting transfers between devices: none -> 22.9 us  [the longest x15 22.5 us: exchange(): arrived.append(lax.ppermute(blocks[shift], 'gx', pairs))]
    psum x2 -> x0, blocking collectives: 22.7 us -> none  [the longest x1 13.5 us: on_device(): square_one = lax.psum(jnp.sum(stream_f * stream_f, axis=1), 'gx')]
    all_to_all x1 -> x2, waiting for transfers between devices: 1.17 us -> 19.9 us  [the longest x1 9.96 us: on_device(): lax.all_to_all(blocks, ('gx', 'gy'), split_axis=0, concat_axis=0, tiled=T...]
    all_gather x3 -> x1, blocking collectives: 26 us -> 8.81 us  [on_device(): rows_in = lax.all_gather(stream_in, 'gy', axis=0, tiled=True)]
  transfers between devices with their start and end apart: 4 -> 20, of which waited for: 2 -> 9; matrix products, arithmetic and copies ran while one was open for 22% -> 2% of each run, Pallas kernels for 0% -> 17%
where the time goes in v1:
time: 137 us
  Pallas kernels  51.4 us (38%)
  waiting for transfers between devices  33.9 us (25%)
  starting transfers between devices  31.6 us (23%)
  blocking collectives  8.81 us (6%)
  local copies, waits for them, and re-layouts  5.92 us (4%)
  other arithmetic  4 us (3%)
    pallas_call x4, Pallas kernels, gate_up_part(): call(functools.partial(mlp_kernel, steps=steps, side=0), 'gate_up_%d' % p...  31.3 us
    ppermute x15, starting transfers between devices, exchange(): arrived.append(lax.ppermute(blocks[shift], 'gx', pairs))  22.5 us
    all_to_all x1, waiting for transfers between devices, on_device(): lax.all_to_all(blocks, ('gx', 'gy'), split_axis=0, concat_axis=0, tiled=T...  9.96 us
    all_to_all x1, waiting for transfers between devices, on_device(): lax.all_to_all(parcel, ('gx', 'gy'), split_axis=0, concat_axis=0, tiled=T...  9.91 us
    all_gather x1, blocking collectives, on_device(): rows_in = lax.all_gather(stream_in, 'gy', axis=0, tiled=True)  8.81 us
    ppermute x15, waiting for transfers between devices, exchange(): arrived.append(lax.ppermute(blocks[shift], 'gx', pairs))  7.1 us
    pallas_call x1, Pallas kernels, project_qkv(): call(functools.partial(qkv_kernel, steps=steps, cut=cut), 'qkv', 4 * coun...  6.54 us
    pallas_call x1, Pallas kernels, project_out(): call(out_kernel, 'out', 2 * count * width * cols, 2 * width * cols, grid=...  5.71 us
  transfers between devices with their start and end apart: 20, of which 9 were waited for; matrix products, arithmetic and copies ran while one was open for 2% of the time, Pallas kernels for 17%

profile of v1, /device:TPU:0, one launch (start us, length us, event | category | flops | bytes accessed | tf_op | source)
XLA Modules:
  0.0 136.6 jit_solution(10009340195498265979)
XLA Ops:
  0.6 8.8 %all_gather.3.rows = bf16[64,2048]{1,0:T(8,128)(2,1)} all-gather(bf16[16,2048]{1,0:T(8,128)(2,1)} %param.9), channel_id=1, replica_groups=mesh['grp'=2,'gx'=4,'gy'=4] {'gy'}, dimensions={0}, use_global_device_ids=true | all-gather | bytes 327680 | tf_op jit(solution)/shard_map/all_gather | solution.py:374
  9.5 6.5 %qkv.1 = bf16[16,4,2432]{2,1,0:T(4,128)(2,1)} custom-call(s32[1]{0:T(128)} %bitcast.2.which, bf16[64,2048]{1,0:T(8,128)(2,1)} %all_gather.3.rows, f32[1,2048]{1,0:T(1,128)} %bitcast.57, bf16[2048,2048]{1,0:T(8,128)(2,1)} %w_query.1, bf16[2048,1024]{1,0:T(8,128)(2,1)} %w_keyval.1), custom_call_target="tpu_custom_call" | custom-call | flops 1207959552 | bytes 9437184 | tf_op jit(solution)/shard_map/qkv/pallas_call | solution.py:85
  16.0 5.1 %all-to-all-start = ((bf16[16,4,2432]{2,1,0:T(4,128)(2,1)}), bf16[16,4,2432]{2,1,0:T(4,128)(2,1)S(1)}, u32[]{:S(2)}, u32[]{:S(2)}) async-start(bf16[16,4,2432]{2,1,0:T(4,128)(2,1)} %qkv.1), calls=%async_computation | async-start | bytes 622592 | tf_op jit(solution)/shard_map/all_to_all | solution.py:378
  22.1 9.9 %all-to-all-done.arrived = bf16[16,4,2432]{2,1,0:T(4,128)(2,1)S(1)} async-done(((bf16[16,4,2432]{2,1,0:T(4,128)(2,1)}), bf16[16,4,2432]{2,1,0:T(4,128)(2,1)S(1)}, u32[]{:S(2)}, u32[]{:S(2)}) %all-to-all-start) | async-done | bytes 311328 | tf_op jit(solution)/shard_map/all_to_all | solution.py:378
  33.2 5.3 %attend.1 = (bf16[4,4,2048]{2,1,0:T(4,128)(2,1)}, bf16[4,1024]{1,0:T(4,128)(2,1)}) custom-call(bf16[16,4,2432]{2,1,0:T(4,128)(2,1)} %copy-done.1, f32[64,128]{1,0:T(8,128)} %bitcast.54, f32[64,128]{1,0:T(8,128)} %bitcast.55, s32[64,1]{1,0:T(8,128)} %tile.32.lengths, bf16[4,2,384,512]{3,2,1,0:T(8,128)(2,1)} %cache.1), custom_call_target="tpu_custom_call" | custom-call | flops 201326592 | bytes 3145728 | tf_op jit(solution)/shard_map/attend/pallas_call | solution.py:192
  38.5 1.7 %broadcast_in_dim.38 = bf16[4,4,4,2048]{3,2,1,0:T(4,128)(2,1)} broadcast(bf16[4,4,2048]{2,1,0:T(4,128)(2,1)} %get-tuple-element.21), dimensions={1,2,3} | broadcast | bytes 327680 | tf_op jit(solution)/shard_map/broadcast_in_dim | solution.py:382
  40.2 3.5 %all-to-all-start.1 = ((bf16[16,4,2048]{2,1,0:T(4,128)(2,1)}), bf16[16,4,2048]{2,1,0:T(4,128)(2,1)S(1)}, u32[]{:S(2)}, u32[]{:S(2)}) async-start(bf16[16,4,2048]{2,1,0:T(4,128)(2,1)} %bitcast.6), calls=%async_computation.1 | async-start | bytes 524288 | tf_op jit(solution)/shard_map/all_to_all | solution.py:384
  43.8 10.0 %all-to-all-done.1 = bf16[16,4,2048]{2,1,0:T(4,128)(2,1)S(1)} async-done(((bf16[16,4,2048]{2,1,0:T(4,128)(2,1)}), bf16[16,4,2048]{2,1,0:T(4,128)(2,1)S(1)}, u32[]{:S(2)}, u32[]{:S(2)}) %all-to-all-start.1) | async-done | bytes 262176 | tf_op jit(solution)/shard_map/all_to_all | solution.py:384
  54.5 5.7 %out.1 = f32[64,2048]{1,0:T(8,128)} custom-call(bf16[64,2048]{1,0:T(8,128)(2,1)} %reshape.80.rows, bf16[2048,2048]{1,0:T(8,128)(2,1)} %weights.1), custom_call_target="tpu_custom_call" | custom-call | flops 536870912 | bytes 8388608 | tf_op jit(solution)/shard_map/out/pallas_call | solution.py:226
  63.0 5.4 %collective-permute-done.1 = bf16[32,2048]{1,0:T(8,128)(2,1)S(1)} collective-permute-done((bf16[32,2048]{1,0:T(8,128)(2,1)S(1)}, bf16[32,2048]{1,0:T(8,128)(2,1)S(1)}, u32[]{:S(2)}, u32[]{:S(2)}) %collective-permute-start.1) | collective-permute-done | bytes 131104 | tf_op jit(solution)/shard_map/ppermute | solution.py:272
  71.1 7.8 %gate_up_0.1 = (bf16[16,3328]{1,0:T(8,128)(2,1)}, bf16[16,3328]{1,0:T(8,128)(2,1)}, bf16[16,3328]{1,0:T(8,128)(2,1)}, bf16[16,3328]{1,0:T(8,128)(2,1)}) custom-call(bf16[64,2176]{1,0:T(8,128)(2,1)} %constant_dynamic-slice_fusion.rows, bf16[2048,52,2,128]{3,2,1,0:T(2,128)(2,1)} %bitcast.47), custom_call_target="tpu_custom_call" | custom-call | flops 872415232 | bytes 13631488 | tf_op jit(solution)/shard_map/gate_up_0/pallas_call | solution.py:313
  80.5 7.8 %gate_up_1.1 = (bf16[16,3328]{1,0:T(8,128)(2,1)}, bf16[16,3328]{1,0:T(8,128)(2,1)}, bf16[16,3328]{1,0:T(8,128)(2,1)}, bf16[16,3328]{1,0:T(8,128)(2,1)}) custom-call(bf16[64,2176]{1,0:T(8,128)(2,1)} %constant_dynamic-slice_fusion.rows, bf16[2048,52,2,128]{3,2,1,0:T(2,128)(2,1)} %bitcast.48), custom_call_target="tpu_custom_call" | custom-call | flops 872415232 | bytes 13631488 | tf_op jit(solution)/shard_map/gate_up_1/pallas_call | solution.py:313
  88.3 2.3 %collective-permute-start.5 = (bf16[16,128]{1,0:T(8,128)(2,1)S(1)}, bf16[16,128]{1,0:T(8,128)(2,1)S(1)}, u32[]{:S(2)}, u32[]{:S(2)}) collective-permute-start(bf16[16,128]{1,0:T(8,128)(2,1)S(1)} %get-tuple-element.42), channel_id=1, source_target_pairs={{0,12},{4,0},{8,4},{12,8},{1,13},{5,1},{9,5},{13,9},{2,14},{6,2},{... | collective-permute-start | bytes 12296 | tf_op jit(solution)/shard_map/ppermute | solution.py:358
  90.6 1.9 %collective-permute-start.4 = (bf16[16,128]{1,0:T(8,128)(2,1)S(1)}, bf16[16,128]{1,0:T(8,128)(2,1)S(1)}, u32[]{:S(2)}, u32[]{:S(2)}) collective-permute-start(bf16[16,128]{1,0:T(8,128)(2,1)S(1)} %get-tuple-element.43), channel_id=1, source_target_pairs={{0,8},{4,12},{8,0},{12,4},{1,9},{5,13},{9,1},{13,5},{2,10},{6,14},... | collective-permute-start | bytes 12296 | tf_op jit(solution)/shard_map/ppermute | solution.py:358
  92.6 7.9 %gate_up_2.1 = (bf16[16,3328]{1,0:T(8,128)(2,1)}, bf16[16,3328]{1,0:T(8,128)(2,1)}, bf16[16,3328]{1,0:T(8,128)(2,1)}, bf16[16,3328]{1,0:T(8,128)(2,1)}) custom-call(bf16[64,2176]{1,0:T(8,128)(2,1)} %constant_dynamic-slice_fusion.rows, bf16[2048,52,2,128]{3,2,1,0:T(2,128)(2,1)} %bitcast.49), custom_call_target="tpu_custom_call" | custom-call | flops 872415232 | bytes 13631488 | tf_op jit(solution)/shard_map/gate_up_2/pallas_call | solution.py:313
  100.5 3.7 %collective-permute-start.8 = (bf16[16,3328]{1,0:T(8,128)(2,1)S(1)}, bf16[16,3328]{1,0:T(8,128)(2,1)S(1)}, u32[]{:S(2)}, u32[]{:S(2)}) collective-permute-start(bf16[16,3328]{1,0:T(8,128)(2,1)S(1)} %copy-done.18), channel_id=1, source_target_pairs={{0,12},{4,0},{8,4},{12,8},{1,13},{5,1},{9,5},{13,9},{2,14},{6,2},{... | collective-permute-start | bytes 319496 | tf_op jit(solution)/shard_map/ppermute | solution.py:358
  104.9 3.3 %collective-permute-start.11 = (bf16[16,3328]{1,0:T(8,128)(2,1)S(1)}, bf16[16,3328]{1,0:T(8,128)(2,1)S(1)}, u32[]{:S(2)}, u32[]{:S(2)}) collective-permute-start(bf16[16,3328]{1,0:T(8,128)(2,1)S(1)} %copy-done.19), channel_id=1, source_target_pairs={{0,12},{4,0},{8,4},{12,8},{1,13},{5,1},{9,5},{13,9},{2,14},{6,2},{... | collective-permute-start | bytes 319496 | tf_op jit(solution)/shard_map/ppermute | solution.py:358
  109.5 7.9 %gate_up_3.1 = (bf16[16,3328]{1,0:T(8,128)(2,1)}, bf16[16,3328]{1,0:T(8,128)(2,1)}, bf16[16,3328]{1,0:T(8,128)(2,1)}, bf16[16,3328]{1,0:T(8,128)(2,1)}) custom-call(bf16[64,2176]{1,0:T(8,128)(2,1)} %constant_dynamic-slice_fusion.rows, bf16[2048,52,2,128]{3,2,1,0:T(2,128)(2,1)} %bitcast.50), custom_call_target="tpu_custom_call" | custom-call | flops 872415232 | bytes 13631488 | tf_op jit(solution)/shard_map/gate_up_3/pallas_call | solution.py:313
  117.4 1.5 %collective-permute-start.13 = (bf16[16,3328]{1,0:T(8,128)(2,1)S(1)}, bf16[16,3328]{1,0:T(8,128)(2,1)S(1)}, u32[]{:S(2)}, u32[]{:S(2)}) collective-permute-start(bf16[16,3328]{1,0:T(8,128)(2,1)S(1)} %copy-done.17), channel_id=1, source_target_pairs={{0,8},{4,12},{8,0},{12,4},{1,9},{5,13},{9,1},{13,5},{2,10},{6,14},... | collective-permute-start | bytes 319496 | tf_op jit(solution)/shard_map/ppermute | solution.py:358
  118.8 3.0 %collective-permute-start.14 = (bf16[16,3328]{1,0:T(8,128)(2,1)S(1)}, bf16[16,3328]{1,0:T(8,128)(2,1)S(1)}, u32[]{:S(2)}, u32[]{:S(2)}) collective-permute-start(bf16[16,3328]{1,0:T(8,128)(2,1)S(1)} %copy-done.16), channel_id=1, source_target_pairs={{0,12},{4,0},{8,4},{12,8},{1,13},{5,1},{9,5},{13,9},{2,14},{6,2},{... | collective-permute-start | bytes 319496 | tf_op jit(solution)/shard_map/ppermute | solution.py:358
  122.8 2.9 %collective-permute-start.17 = (bf16[16,3328]{1,0:T(8,128)(2,1)}, bf16[16,3328]{1,0:T(8,128)(2,1)S(1)}, u32[]{:S(2)}, u32[]{:S(2)}) collective-permute-start(bf16[16,3328]{1,0:T(8,128)(2,1)} %get-tuple-element.37), channel_id=1, source_target_pairs={{0,12},{4,0},{8,4},{12,8},{1,13},{5,1},{9,5},{13,9},{2,14},{6,2},{... | collective-permute-start | bytes 319496 | tf_op jit(solution)/shard_map/ppermute | solution.py:358
  127.4 2.7 %collective-permute-done.15.refs_13_ = bf16[16,3328]{1,0:T(8,128)(2,1)S(1)} collective-permute-done((bf16[16,3328]{1,0:T(8,128)(2,1)}, bf16[16,3328]{1,0:T(8,128)(2,1)S(1)}, u32[]{:S(2)}, u32[]{:S(2)}) %collective-permute-start.15) | collective-permute-done | bytes 106528 | tf_op jit(solution)/shard_map/ppermute | solution.py:358
  130.1 3.3 %collective-permute-done.16.refs_14_ = bf16[16,3328]{1,0:T(8,128)(2,1)S(1)} collective-permute-done((bf16[16,3328]{1,0:T(8,128)(2,1)}, bf16[16,3328]{1,0:T(8,128)(2,1)S(1)}, u32[]{:S(2)}, u32[]{:S(2)}) %collective-permute-start.16) | collective-permute-done | bytes 106528 | tf_op jit(solution)/shard_map/ppermute | solution.py:358
  134.1 2.5 %hidden.1 = bf16[16,6656]{1,0:T(8,128)(2,1)} custom-call(bf16[4,16,128]{2,1,0:T(8,128)(2,1)} %pad_maximum_fusion.1.sides, bf16[16,3328]{1,0:T(8,128)(2,1)} %get-tuple-element.22.refs_0_, bf16[16,3328]{1,0:T(8,128)(2,1)} %copy-done.2, bf16[16,3328]{1,0:T(8,128)(2,1)} %copy-done.3, bf16[16,3328]{1,0:T(8,128)(2,1)} %copy-done.4, ...), custom_call_target="tpu_custom_call" | custom-call | flops 3407872 | bytes 1703936 | tf_op jit(solution)/shard_map/hidden/pallas_call | solution.py:402
  (104 shorter events, 15.3 us)
Async XLA Ops:
  0.6 20.5 %copy-start.15 = (s32[4]{0:T(128)S(1)}, s32[4]{0:T(128)}, u32[]{:S(2)}) copy-start(s32[4]{0:T(128)} %param.17) | copy-start | bytes 52
  9.5 34.3 %copy-start = (bf16[64,2048]{1,0:T(8,128)(2,1)S(1)}, bf16[64,2048]{1,0:T(8,128)(2,1)}, u32[]{:S(2)}) copy-start(bf16[64,2048]{1,0:T(8,128)(2,1)} %all_gather.3.rows) | copy-start | bytes 786436
  16.0 52.4 %copy-start.14 = (f32[2048]{0:T(1024)S(1)}, f32[2048]{0:T(1024)}, u32[]{:S(2)}) copy-start(f32[2048]{0:T(1024)} %param.11) | copy-start | bytes 24580
  16.0 16.0 %all-to-all-start = ((bf16[16,4,2432]{2,1,0:T(4,128)(2,1)}), bf16[16,4,2432]{2,1,0:T(4,128)(2,1)S(1)}, u32[]{:S(2)}, u32[]{:S(2)}) async-start(bf16[16,4,2432]{2,1,0:T(4,128)(2,1)} %qkv.1), calls=%async_computation | async-start | bytes 622592 | tf_op jit(solution)/shard_map/all_to_all | solution.py:378
  40.2 13.5 %all-to-all-start.1 = ((bf16[16,4,2048]{2,1,0:T(4,128)(2,1)}), bf16[16,4,2048]{2,1,0:T(4,128)(2,1)S(1)}, u32[]{:S(2)}, u32[]{:S(2)}) async-start(bf16[16,4,2048]{2,1,0:T(4,128)(2,1)} %bitcast.6), calls=%async_computation.1 | async-start | bytes 524288 | tf_op jit(solution)/shard_map/all_to_all | solution.py:384
  61.3 1.4 %collective-permute-start = (bf16[32,2048]{1,0:T(8,128)(2,1)S(1)}, bf16[32,2048]{1,0:T(8,128)(2,1)S(1)}, u32[]{:S(2)}, u32[]{:S(2)}) collective-permute-start(bf16[32,2048]{1,0:T(8,128)(2,1)S(1)} %bitcast.56), channel_id=1, source_target_pairs={{0,1},{1,0},{2,3},{3,2},{4,5},{5,4},{6,7},{7,6},{8,9},{9,8},{10,11... | collective-permute-start | bytes 393224 | tf_op jit(solution)/shard_map/ppermute | solution.py:271
  62.7 5.7 %collective-permute-start.1 = (bf16[32,2048]{1,0:T(8,128)(2,1)S(1)}, bf16[32,2048]{1,0:T(8,128)(2,1)S(1)}, u32[]{:S(2)}, u32[]{:S(2)}) collective-permute-start(bf16[32,2048]{1,0:T(8,128)(2,1)S(1)} %fusion.1), channel_id=1, source_target_pairs={{0,2},{2,0},{1,3},{3,1},{4,6},{6,4},{5,7},{7,5},{8,10},{10,8},{9,1... | collective-permute-start | bytes 393224 | tf_op jit(solution)/shard_map/ppermute | solution.py:272
  68.8 1.4 %collective-permute-start.2 = (bf16[32,2176]{1,0:T(8,128)(2,1)S(1)}, bf16[32,2176]{1,0:T(8,128)(2,1)S(1)}, u32[]{:S(2)}, u32[]{:S(2)}) collective-permute-start(bf16[32,2176]{1,0:T(8,128)(2,1)S(1)} %pad_maximum_fusion), channel_id=1, source_target_pairs={{0,1},{1,0},{2,3},{3,2},{4,5},{5,4},{6,7},{7,6},{8,9},{9,8},{10,11... | collective-permute-start | bytes 417800 | tf_op jit(solution)/shard_map/ppermute | solution.py:278
  78.9 26.1 %collective-permute-start.6 = (bf16[16,3328]{1,0:T(8,128)(2,1)}, bf16[16,3328]{1,0:T(8,128)(2,1)S(1)}, u32[]{:S(2)}, u32[]{:S(2)}) collective-permute-start(bf16[16,3328]{1,0:T(8,128)(2,1)} %get-tuple-element.23), channel_id=1, source_target_pairs={{0,4},{4,8},{8,12},{12,0},{1,5},{5,9},{9,13},{13,1},{2,6},{6,10},{... | collective-permute-start | bytes 319496 | tf_op jit(solution)/shard_map/ppermute | solution.py:358
  79.3 28.9 %collective-permute-start.7 = (bf16[16,3328]{1,0:T(8,128)(2,1)}, bf16[16,3328]{1,0:T(8,128)(2,1)S(1)}, u32[]{:S(2)}, u32[]{:S(2)}) collective-permute-start(bf16[16,3328]{1,0:T(8,128)(2,1)} %get-tuple-element.24), channel_id=1, source_target_pairs={{0,8},{4,12},{8,0},{12,4},{1,9},{5,13},{9,1},{13,5},{2,10},{6,14},... | collective-permute-start | bytes 319496 | tf_op jit(solution)/shard_map/ppermute | solution.py:358
  88.3 12.2 %collective-permute-start.5 = (bf16[16,128]{1,0:T(8,128)(2,1)S(1)}, bf16[16,128]{1,0:T(8,128)(2,1)S(1)}, u32[]{:S(2)}, u32[]{:S(2)}) collective-permute-start(bf16[16,128]{1,0:T(8,128)(2,1)S(1)} %get-tuple-element.42), channel_id=1, source_target_pairs={{0,12},{4,0},{8,4},{12,8},{1,13},{5,1},{9,5},{13,9},{2,14},{6,2},{... | collective-permute-start | bytes 12296 | tf_op jit(solution)/shard_map/ppermute | solution.py:358
  90.6 13.6 %collective-permute-start.4 = (bf16[16,128]{1,0:T(8,128)(2,1)S(1)}, bf16[16,128]{1,0:T(8,128)(2,1)S(1)}, u32[]{:S(2)}, u32[]{:S(2)}) collective-permute-start(bf16[16,128]{1,0:T(8,128)(2,1)S(1)} %get-tuple-element.43), channel_id=1, source_target_pairs={{0,8},{4,12},{8,0},{12,4},{1,9},{5,13},{9,1},{13,5},{2,10},{6,14},... | collective-permute-start | bytes 12296 | tf_op jit(solution)/shard_map/ppermute | solution.py:358
  92.6 11.7 %collective-permute-start.3 = (bf16[16,128]{1,0:T(8,128)(2,1)S(1)}, bf16[16,128]{1,0:T(8,128)(2,1)S(1)}, u32[]{:S(2)}, u32[]{:S(2)}) collective-permute-start(bf16[16,128]{1,0:T(8,128)(2,1)S(1)} %get-tuple-element.44), channel_id=1, source_target_pairs={{0,4},{4,8},{8,12},{12,0},{1,5},{5,9},{9,13},{13,1},{2,6},{6,10},{... | collective-permute-start | bytes 12296 | tf_op jit(solution)/shard_map/ppermute | solution.py:358
  100.5 16.8 %collective-permute-start.8 = (bf16[16,3328]{1,0:T(8,128)(2,1)S(1)}, bf16[16,3328]{1,0:T(8,128)(2,1)S(1)}, u32[]{:S(2)}, u32[]{:S(2)}) collective-permute-start(bf16[16,3328]{1,0:T(8,128)(2,1)S(1)} %copy-done.18), channel_id=1, source_target_pairs={{0,12},{4,0},{8,4},{12,8},{1,13},{5,1},{9,5},{13,9},{2,14},{6,2},{... | collective-permute-start | bytes 319496 | tf_op jit(solution)/shard_map/ppermute | solution.py:358
  104.3 14.6 %collective-permute-start.9 = (bf16[16,3328]{1,0:T(8,128)(2,1)S(1)}, bf16[16,3328]{1,0:T(8,128)(2,1)S(1)}, u32[]{:S(2)}, u32[]{:S(2)}) collective-permute-start(bf16[16,3328]{1,0:T(8,128)(2,1)S(1)} %copy-done.21), channel_id=1, source_target_pairs={{0,4},{4,8},{8,12},{12,0},{1,5},{5,9},{9,13},{13,1},{2,6},{6,10},{... | collective-permute-start | bytes 319496 | tf_op jit(solution)/shard_map/ppermute | solution.py:358
  104.3 17.5 %collective-permute-start.10 = (bf16[16,3328]{1,0:T(8,128)(2,1)S(1)}, bf16[16,3328]{1,0:T(8,128)(2,1)S(1)}, u32[]{:S(2)}, u32[]{:S(2)}) collective-permute-start(bf16[16,3328]{1,0:T(8,128)(2,1)S(1)} %copy-done.20), channel_id=1, source_target_pairs={{0,8},{4,12},{8,0},{12,4},{1,9},{5,13},{9,1},{13,5},{2,10},{6,14},... | collective-permute-start | bytes 319496 | tf_op jit(solution)/shard_map/ppermute | solution.py:358
  104.9 16.9 %collective-permute-start.11 = (bf16[16,3328]{1,0:T(8,128)(2,1)S(1)}, bf16[16,3328]{1,0:T(8,128)(2,1)S(1)}, u32[]{:S(2)}, u32[]{:S(2)}) collective-permute-start(bf16[16,3328]{1,0:T(8,128)(2,1)S(1)} %copy-done.19), channel_id=1, source_target_pairs={{0,12},{4,0},{8,4},{12,8},{1,13},{5,1},{9,5},{13,9},{2,14},{6,2},{... | collective-permute-start | bytes 319496 | tf_op jit(solution)/shard_map/ppermute | solution.py:358
  108.2 14.6 %collective-permute-start.12 = (bf16[16,3328]{1,0:T(8,128)(2,1)}, bf16[16,3328]{1,0:T(8,128)(2,1)S(1)}, u32[]{:S(2)}, u32[]{:S(2)}) collective-permute-start(bf16[16,3328]{1,0:T(8,128)(2,1)} %get-tuple-element.31), channel_id=1, source_target_pairs={{0,4},{4,8},{8,12},{12,0},{1,5},{5,9},{9,13},{13,1},{2,6},{6,10},{... | collective-permute-start | bytes 319496 | tf_op jit(solution)/shard_map/ppermute | solution.py:358
  117.3 16.1 %copy-start.4 = (bf16[16,3328]{1,0:T(8,128)(2,1)}, bf16[16,3328]{1,0:T(8,128)(2,1)S(1)}, u32[]{:S(2)}) copy-start(bf16[16,3328]{1,0:T(8,128)(2,1)S(1)} %collective-permute-done.8.refs_3_) | copy-start | bytes 319492
  117.4 9.6 %collective-permute-start.13 = (bf16[16,3328]{1,0:T(8,128)(2,1)S(1)}, bf16[16,3328]{1,0:T(8,128)(2,1)S(1)}, u32[]{:S(2)}, u32[]{:S(2)}) collective-permute-start(bf16[16,3328]{1,0:T(8,128)(2,1)S(1)} %copy-done.17), channel_id=1, source_target_pairs={{0,8},{4,12},{8,0},{12,4},{1,9},{5,13},{9,1},{13,5},{2,10},{6,14},... | collective-permute-start | bytes 319496 | tf_op jit(solution)/shard_map/ppermute | solution.py:358
  118.8 8.5 %collective-permute-start.14 = (bf16[16,3328]{1,0:T(8,128)(2,1)S(1)}, bf16[16,3328]{1,0:T(8,128)(2,1)S(1)}, u32[]{:S(2)}, u32[]{:S(2)}) collective-permute-start(bf16[16,3328]{1,0:T(8,128)(2,1)S(1)} %copy-done.16), channel_id=1, source_target_pairs={{0,12},{4,0},{8,4},{12,8},{1,13},{5,1},{9,5},{13,9},{2,14},{6,2},{... | collective-permute-start | bytes 319496 | tf_op jit(solution)/shard_map/ppermute | solution.py:358
  121.8 8.3 %collective-permute-start.15 = (bf16[16,3328]{1,0:T(8,128)(2,1)}, bf16[16,3328]{1,0:T(8,128)(2,1)S(1)}, u32[]{:S(2)}, u32[]{:S(2)}) collective-permute-start(bf16[16,3328]{1,0:T(8,128)(2,1)} %get-tuple-element.35), channel_id=1, source_target_pairs={{0,4},{4,8},{8,12},{12,0},{1,5},{5,9},{9,13},{13,1},{2,6},{6,10},{... | collective-permute-start | bytes 319496 | tf_op jit(solution)/shard_map/ppermute | solution.py:358
  121.8 11.6 %collective-permute-start.16 = (bf16[16,3328]{1,0:T(8,128)(2,1)}, bf16[16,3328]{1,0:T(8,128)(2,1)S(1)}, u32[]{:S(2)}, u32[]{:S(2)}) collective-permute-start(bf16[16,3328]{1,0:T(8,128)(2,1)} %get-tuple-element.36), channel_id=1, source_target_pairs={{0,8},{4,12},{8,0},{12,4},{1,9},{5,13},{9,1},{13,5},{2,10},{6,14},... | collective-permute-start | bytes 319496 | tf_op jit(solution)/shard_map/ppermute | solution.py:358
  122.8 10.6 %collective-permute-start.17 = (bf16[16,3328]{1,0:T(8,128)(2,1)}, bf16[16,3328]{1,0:T(8,128)(2,1)S(1)}, u32[]{:S(2)}, u32[]{:S(2)}) collective-permute-start(bf16[16,3328]{1,0:T(8,128)(2,1)} %get-tuple-element.37), channel_id=1, source_target_pairs={{0,12},{4,0},{8,4},{12,8},{1,13},{5,1},{9,5},{13,9},{2,14},{6,2},{... | collective-permute-start | bytes 319496 | tf_op jit(solution)/shard_map/ppermute | solution.py:358
  (18 other events, 149.5 us)
